TPU v7x, 768 devices: a whole 4x8x12 slice. The times are simulated.
768 devices in a mesh: mp: 48 (over y, z_hi, core), tokens: 16 (over z_lo, x).
Axes of the slice: x: 4, y: 8, z: 12 (z_hi: 3, z_lo: 4; z = z_hi * 4 + z_lo), core: 2. Of those that a mesh axis runs over, the one named last changes fastest.
Arguments:
- tokens_in: bfloat16 [3072, 5120], P(('tokens', 'mp')), may hold values from -6 to 6
- grad_out: bfloat16 [3072, 5120], P(('tokens', 'mp')), may hold values from -6 to 6
- pre_act: bfloat16 [3072, 13824], P('tokens', 'mp'), may hold values from -6 to 6
- w_in: bfloat16 [5120, 13824], P(None, 'mp'), may hold values from -0.078125 to 0.078125
- w_out: bfloat16 [13824, 5120], P('mp'), may hold values from -0.0546875 to 0.0546875
Outputs:
- grad_in: bfloat16 [3072, 5120], P(('tokens', 'mp'))
- grad_w_in: bfloat16 [5120, 13824], P('tokens', 'mp')
- grad_w_out: bfloat16 [13824, 5120], P('mp', 'tokens')
All inputs are finite; a program needn't handle non-finite values.
Results may differ from a plain program's by a relative error of at most 0.023.
Values may be sent and summed in bfloat16 or wider, within the bound.
A program may use at most 64 MiB of HBM per device.

v0:
```python
import math

import jax
import jax.numpy as jnp
from jax import lax
from jax.sharding import PartitionSpec as P

root_two_pi = math.sqrt(2.0 / math.pi)
cubic = 0.044715


def gelu_value(pre):
    inner = root_two_pi * (pre + cubic * pre * pre * pre)
    return 0.5 * pre * (1.0 + jnp.tanh(inner))


def gelu_slope(pre):
    tanh_val = jnp.tanh(root_two_pi * (pre + cubic * pre * pre * pre))
    return 0.5 * (1.0 + tanh_val) + 0.5 * pre * (1.0 - tanh_val * tanh_val) * root_two_pi * (
        1.0 + 3.0 * cubic * pre * pre
    )


def shards(tokens_in, grad_out, pre_act, w_in, w_out):
    rows_in, rows_grad = (
        lax.all_gather(tokens_in, "mp", axis=0, tiled=True),
        lax.all_gather(grad_out, "mp", axis=0, tiled=True),
    )
    pre = pre_act.astype(jnp.float32)
    activated = gelu_value(pre).astype(jnp.bfloat16)
    slope = gelu_slope(pre)
    grad_act = lax.dot_general(
        rows_grad, w_out, (((1,), (1,)), ((), ())), preferred_element_type=jnp.float32
    )
    grad_pre = (grad_act * slope).astype(jnp.bfloat16)
    grad_in = lax.psum_scatter(
        lax.dot_general(
            grad_pre, w_in, (((1,), (1,)), ((), ())), preferred_element_type=jnp.float32
        ),
        "mp",
        scatter_dimension=0,
        tiled=True,
    ).astype(jnp.bfloat16)
    group_count = lax.axis_size("tokens")
    total = rows_in.shape[0] * group_count
    scale_back = 1.0 / math.sqrt(total)
    part_in = (
        lax.dot_general(
            rows_in, grad_pre, (((0,), (0,)), ((), ())), preferred_element_type=jnp.float32
        )
        * scale_back
    )
    part_out = (
        lax.dot_general(
            activated, rows_grad, (((0,), (0,)), ((), ())), preferred_element_type=jnp.float32
        )
        * scale_back
    )
    sum_in, sum_out = (
        lax.psum_scatter(
            part_in.astype(jnp.bfloat16), "tokens", scatter_dimension=0, tiled=True
        ).astype(jnp.float32),
        lax.psum_scatter(
            part_out.astype(jnp.bfloat16), "tokens", scatter_dimension=1, tiled=True
        ).astype(jnp.float32),
    )
    grad_w_in = sum_in.astype(jnp.bfloat16)
    grad_w_out = sum_out.astype(jnp.bfloat16)
    return (grad_in, grad_w_in, grad_w_out)


def solution(mesh):
    placed = (
        P(("tokens", "mp"), None),
        P(("tokens", "mp"), None),
        P("tokens", "mp"),
        P(None, "mp"),
        P("mp", None),
    )
    return jax.shard_map(
        shards,
        mesh=mesh,
        in_specs=placed,
        out_specs=(P(("tokens", "mp"), None), P("tokens", "mp"), P("mp", "tokens")),
        check_vma=False,
    )
```

profile of v0, /device:TPU:128, one launch (start us, length us, event | category | flops | bytes accessed | tf_op | source)
XLA Modules:
  0.0 609.7 jit_solution(10547485216085986923)
XLA Ops:
  7.2 0.0 copy-start
  7.2 0.0 copy-start.2
  7.2 0.0 all-gather.5.cloned.1.call-start
  7.2 0.7 all-gather.5.cloned.1.call-update
  7.9 0.0 all-gather.7.cloned.1.call-start
  8.0 0.7 all-gather.7.cloned.1.call-update
  8.7 0.0 reduce-scatter.9.cloned.1.call-start
  8.7 109.4 %all-gather.5.cloned.1.call-done = bf16[48,4,5120]{2,1,0:T(4,128)(2,1)} async-done(((bf16[1,4,5120]{2,1,0:T(4,128)(2,1)}), bf16[48,4,5120]{2,1,0:T(4,128)(2,1)}) %all-gather.5.cloned.1.call-update) | async-done | bytes 1966096 | tf_op jit(solution)/shard_map/all_gather | solution.py:27
  118.2 4.1 reshape.7
  122.3 0.0 copy-done.2
  122.3 4.2 fusion.1
  126.4 5.7 copy.10
  132.1 0.0 reduce-scatter.9.cloned.1.call-update
  132.1 0.0 reduce-scatter.7.cloned.1.call-start
  132.2 87.5 %all-gather.7.cloned.1.call-done = bf16[48,4,5120]{2,1,0:T(4,128)(2,1)} async-done(((bf16[1,4,5120]{2,1,0:T(4,128)(2,1)}), bf16[48,4,5120]{2,1,0:T(4,128)(2,1)}) %all-gather.7.cloned.1.call-update) | async-done | bytes 1966096 | tf_op jit(solution)/shard_map/all_gather | solution.py:26
  219.7 4.1 reshape.9
  223.8 0.0 copy-start.1
  223.8 4.1 fusion.3
  227.9 0.0 copy-done.1
  227.9 2.7 fusion.2
  230.5 5.7 copy.8
  236.2 0.0 reduce-scatter.7.cloned.1.call-update
  236.2 1.3 dynamic-slice
  238.2 0.0 copy-done
  238.2 3.2 fusion.22
  241.3 356.7 %all-reduce.2 = bf16[192,5120]{1,0:T(8,128)(2,1)} all-reduce(f32[192,5120]{1,0:T(8,128)} %fusion.22), channel_id=2, replica_groups=mesh['mp'=48,'tokens'=16] {'mp'}, use_global_device_ids=true, to_apply=%region_0.0.clone | all-reduce | flops 983040 | bytes 5898240
  598.1 1.5 dynamic-slice_convert_fusion
  599.6 0.0 reduce-scatter.9.cloned.1.call-done
  599.6 1.8 copy.11
  601.4 0.0 reduce-scatter.7.cloned.1.call-done
  601.4 1.8 copy.9
Async XLA Ops:
  7.2 231.0 %copy-start = (bf16[5120,288]{0,1:T(8,128)(2,1)S(1)}, bf16[5120,288]{0,1:T(8,128)(2,1)}, u32[]{:S(2)}) copy-start(bf16[5120,288]{0,1:T(8,128)(2,1)} %param.8) | copy-start | bytes 8847364
  7.2 115.1 %copy-start.2 = (bf16[192,288]{1,0:T(8,128)(2,1)S(1)}, bf16[192,288]{1,0:T(8,128)(2,1)}, u32[]{:S(2)}) copy-start(bf16[192,288]{1,0:T(8,128)(2,1)} %param.7) | copy-start | bytes 331780
  7.2 111.0 %all-gather.5.cloned.1.call-start = ((), (), s32[]{:S(2)}) async-start(), calls=%async_computation.2 | async-start | bytes 2007040 | tf_op jit(solution)/shard_map/all_gather | solution.py:27
  7.9 211.8 %all-gather.7.cloned.1.call-start = ((), (), s32[]{:S(2)}) async-start(), calls=%async_computation.3 | async-start | bytes 2007040 | tf_op jit(solution)/shard_map/all_gather | solution.py:26
  8.7 590.9 %reduce-scatter.9.cloned.1.call-start = ((), (), s32[]{:S(2)}) async-start(), calls=%async_computation.5 | async-start | bytes 4177920
  132.1 469.3 %reduce-scatter.7.cloned.1.call-start = ((), (), s32[]{:S(2)}) async-start(), calls=%async_computation.4 | async-start | bytes 4177920
  223.8 4.1 copy-start.1
Sparse Core Ops, SparseCore 0:
  12.1 106.0 all-gather.4
  122.2 97.4 all-gather.6
  222.9 94.1 reduce-scatter.8
  320.4 125.6 reduce-scatter.6
where the time goes:
time: 610 us
  blocking collectives  357 us (59%)
  waiting for transfers between devices  198 us (32%)
  local copies, waits for them, and re-layouts  25.9 us (4%)
  between operations  14.5 us (2%)
  matrix products  14.1 us (2%)
    unnamed x1, blocking collectives  357 us
    all_gather x1, waiting for transfers between devices, shards(): lax.all_gather(grad_out, 'mp', axis=0, tiled=True)  109 us
    all_gather x1, waiting for transfers between devices, shards(): lax.all_gather(tokens_in, 'mp', axis=0, tiled=True)  87.5 us
    unnamed x13, local copies, waits for them, and re-layouts  24.3 us
  transfers between devices with their start and end apart: 4, of which 2 were waited for; matrix products, arithmetic and copies ran while one was open for 6% of the time, Pallas kernels for 0%

commit v1 on v0

v1 whole, which is shorter than its diff:
```python
import math

import jax
import jax.numpy as jnp
from jax import lax
from jax.experimental import pallas as pl
from jax.experimental.pallas import tpu as pltpu
from jax.sharding import PartitionSpec as P

root_two_pi = math.sqrt(2.0 / math.pi)
cubic = 0.044715

NY, NZ, NC = 8, 3, 2
NL, NX = 4, 4
ROWS = 4
BLK = ROWS * NX
NB = NY * NZ
NBLK = NC * NB
QB = NBLK // NX
QR = QB * BLK
WIDE = 5120
HID = 288
DQ = WIDE // NX
DP = DQ // NL
WIN = 384
MESH = pl.DeviceIdType.MESH
f32 = jnp.float32
bf16 = jnp.bfloat16


def gelu_value(pre):
    inner = root_two_pi * (pre + cubic * pre * pre * pre)
    return 0.5 * pre * (1.0 + jnp.tanh(inner))


def gelu_slope(pre):
    tanh_val = jnp.tanh(root_two_pi * (pre + cubic * pre * pre * pre))
    return 0.5 * (1.0 + tanh_val) + 0.5 * pre * (1.0 - tanh_val * tanh_val) * root_two_pi * (
        1.0 + 3.0 * cubic * pre * pre
    )


def kernel(
    go_ref, ti_ref, pre_ref, wo_ref, wi_ref,
    gin_ref, gwi_ref, gwo_ref,
    xsrc, xbuf, mbuf, gbuf, wwin, wsel, prebuf, pref, act, pbuf, gaown, rsbuf, gpbuf,
    wchunk, wrecv, gown, gsend, grecv, rsend, rrecv, zown, zsend, zrecv, fbuf, osrc, obuf,
    send_sem, x_sem, pre_sem, zg_sem, y_sem, sib_sem, w_sem, rs_sem, ag_sem, wr_sem,
    gs_sem, ry_sem, rz_sem, ro_sem,
):
    m = lax.axis_index("mp")
    t = lax.axis_index("tokens")
    c = lax.rem(m, NC)
    zh = lax.rem(m // NC, NZ)
    y = m // (NC * NZ)
    x = lax.rem(t, NX)
    zl = t // NX
    sg = 1 - 2 * c

    def at(y_=None, zh_=None, c_=None, zl_=None, x_=None):
        y_ = y if y_ is None else y_
        zh_ = zh if zh_ is None else zh_
        c_ = c if c_ is None else c_
        zl_ = zl if zl_ is None else zl_
        x_ = x if x_ is None else x_
        return {"mp": (y_ * NZ + zh_) * NC + c_, "tokens": zl_ * NX + x_}

    def ring(v, n):
        return lax.rem(v + n, n)

    other = 1 - c
    xs = [lax.rem(x + d, NX) for d in range(1, NX)]
    zhs = [lax.rem(zh + d, NZ) for d in range(1, NZ)]
    zls = [lax.rem(zl + d, NL) for d in range(1, NL)]
    fwd = at(y_=ring(y + sg, NY))
    bwd = at(y_=ring(y - sg, NY))
    sib = at(c_=other)
    flying = []

    def send(src, dst, sem, dev):
        cp = pltpu.make_async_remote_copy(
            src_ref=src, dst_ref=dst, send_sem=send_sem.at[len(flying)], recv_sem=sem,
            device_id=dev, device_id_type=MESH,
        )
        cp.start()
        flying.append(cp)

    def arrive(dst, sem):
        pltpu.make_async_remote_copy(
            src_ref=dst, dst_ref=dst, send_sem=send_sem.at[0], recv_sem=sem,
            device_id=sib, device_id_type=MESH,
        ).wait_recv()

    base = x * DP
    low = pl.multiple_of((base // 128) * 128, 128)
    odd = lax.rem(x, 2)
    loads = []
    for i, w in enumerate((wo_ref, wi_ref)):
        for k in range(NL):
            cp = pltpu.make_async_copy(
                w.at[:, pl.ds(pl.multiple_of(low + k * DQ, 128), WIN)], wwin.at[i, k], w_sem.at[i, k]
            )
            cp.start()
            loads.append(cp)

    for a, ref in enumerate((go_ref, ti_ref)):
        v = ref[...].astype(f32)
        for p in range(NX):
            xsrc[a, p] = jnp.concatenate(
                [v[:, k * DQ + p * DP : k * DQ + (p + 1) * DP] for k in range(NL)], axis=1
            ).astype(bf16)

    barrier = pltpu.get_barrier_semaphore()
    peers = (
        [at(x_=v) for v in xs] + [at(zh_=v) for v in zhs] + [at(zl_=v) for v in zls]
        + [fwd, bwd, sib]
    )
    for dev in peers:
        pl.semaphore_signal(barrier, inc=1, device_id=dev, device_id_type=MESH)
    pl.semaphore_wait(barrier, len(peers))

    for a in range(2):
        for v in xs:
            send(xsrc.at[a, v], xbuf.at[a, x], x_sem.at[a, x], at(x_=v))
    for v in xs:
        send(pre_ref, prebuf.at[x], pre_sem.at[x], at(x_=v))

    def block(y_, zh_, c_):
        return c_ * NB + y_ * NZ + zh_

    def merge(a):
        for v in xs:
            arrive(xbuf.at[a, v], x_sem.at[a, v])
        xbuf[a, pl.ds(x, 1)] = xsrc[a, pl.ds(x, 1)]
        for p in range(NX):
            mbuf[ROWS * p : ROWS * (p + 1)] = xbuf[a, p].astype(f32)
        gbuf[a, pl.ds(block(y, zh, c), 1)] = mbuf[...].astype(bf16)[None]
        mine = gbuf.at[a, block(y, zh, c)]
        for i, v in enumerate(zhs):
            send(mine, mine, zg_sem.at[a, zh], at(zh_=v))

    def hop(a, d, s, y_, zh_):
        ref = gbuf.at[a, block(y_, zh_, c)]
        send(ref, ref, y_sem.at[a, d, s, zh_], fwd if d == 0 else bwd)

    def to_sib(a, y_):
        ref = gbuf.at[a, pl.ds(block(y_, 0, c), NZ)]
        send(ref, ref, sib_sem.at[a, y_], sib)

    order = [zh] + zhs
    hops = (NY // 2, NY // 2 - 1)

    def ring_first(a, i):
        v = order[i]
        if i:
            ref = gbuf.at[a, block(y, v, c)]
            arrive(ref, zg_sem.at[a, v])
        hop(a, 0, 0, y, v)
        hop(a, 1, 0, y, v)
        if i == NZ - 1:
            to_sib(a, y)

    def ring_step(a, s):
        for i in range(NZ):
            v = order[i]
            for d in range(2):
                if s <= hops[d]:
                    y_ = ring(y - s * sg if d == 0 else y + s * sg, NY)
                    arrive(gbuf.at[a, block(y_, v, c)], y_sem.at[a, d, s - 1, v])
                    if s < hops[d]:
                        hop(a, d, s, y_, v)
                    if i == NZ - 1:
                        to_sib(a, y_)

    def ring_end(a):
        for y_ in range(NY):
            arrive(gbuf.at[a, pl.ds(block(y_, 0, other), NZ)], sib_sem.at[a, y_])

    merge(0)
    ring_first(0, 0)
    merge(1)
    ring_first(0, 1)
    ring_first(0, 2)

    for cp in loads:
        cp.wait()
    for i in range(2):
        parts = []
        for k in range(NL):
            v = wwin[i, k].astype(f32)
            turned = pltpu.roll(v, WIN - DP % 128, 1)
            parts.append(jnp.where(odd == 1, turned, v)[:, :DP])
        wsel[i] = jnp.concatenate(parts, axis=1).astype(bf16)

    ring_step(0, 1)

    for v in xs:
        arrive(prebuf.at[v], pre_sem.at[v])
    prebuf[pl.ds(x, 1)] = pre_ref[...][None]

    def pre_rows(q, carry):
        i = lax.broadcasted_iota(jnp.int32, (QR, QR), 0)
        j = lax.broadcasted_iota(jnp.int32, (QR, QR), 1)
        yz = QB * lax.rem(q, NX // NC) + (i >> 4)
        src = (yz * NC + q // (NX // NC)) * ROWS + (i & 3)
        total = jnp.zeros((QR, HID), f32)
        for p in range(NX):
            hot = jnp.where((src == j) & (((i >> 2) & 3) == p), 1.0, 0.0).astype(bf16)
            total += jnp.dot(hot, prebuf[p], preferred_element_type=f32)
        pref[q] = total
        act[q] = gelu_value(total).astype(bf16)
        return carry

    lax.fori_loop(0, NX, pre_rows, 0)

    ring_step(0, 2)
    ring_step(0, 3)
    ring_step(0, 4)
    ring_end(0)

    def rows_of(a, q):
        return gbuf[a, pl.ds(QB * q, QB)].reshape(QR, DQ)

    for v in xs + [x]:
        part = lax.dot_general(
            rows_of(0, v), wsel[0], (((1,), (1,)), ((), ())), preferred_element_type=f32
        )
        if v is x:
            gaown[...] = part
        else:
            pbuf[pl.ds(v, 1)] = part.astype(bf16)[None]
            send(pbuf.at[v], rsbuf.at[x], rs_sem.at[x], at(x_=v))
    for i in range(NZ):
        ring_first(1, i)

    scale_back = 1.0 / math.sqrt(NL * NX * NC * NB * ROWS)

    def weight_part(a, left):
        lhs = left[...].reshape(NX * QR, HID)
        for h in range(2):
            cols = 2 * DP
            right = gbuf[a, :, :, h * cols : (h + 1) * cols].reshape(NX * QR, cols)
            part = (
                lax.dot_general(lhs, right, (((0,), (0,)), ((), ())), preferred_element_type=f32)
                * scale_back
            ).astype(bf16)
            wchunk[a, 2 * h] = part[:, :DP]
            wchunk[a, 2 * h + 1] = part[:, DP:]
        for v in zls:
            send(wchunk.at[a, v], wrecv.at[a, zl], wr_sem.at[a, zl], at(zl_=v))

    def weight_sum(a, out):
        total = wchunk[a, pl.ds(zl, 1)][0].astype(f32)
        for v in zls:
            arrive(wrecv.at[a, v], wr_sem.at[a, v])
            total += wrecv[a, pl.ds(v, 1)][0].astype(f32)
        out[...] = total.astype(bf16)

    weight_part(0, act)
    ring_step(1, 1)

    total = gaown[...]
    for v in xs:
        arrive(rsbuf.at[v], rs_sem.at[v])
        total += rsbuf[pl.ds(v, 1)][0].astype(f32)
    grad_pre = (total * gelu_slope(pref[pl.ds(x, 1)][0])).astype(bf16)
    gpbuf[pl.ds(x, 1)] = grad_pre[None]
    for v in xs:
        send(gpbuf.at[x], gpbuf.at[x], ag_sem.at[x], at(x_=v))

    ring_step(1, 2)
    ring_step(1, 3)
    ring_step(1, 4)

    for v in xs:
        arrive(gpbuf.at[v], ag_sem.at[v])

    def in_part(first, keep):
        for h in range(2):
            part = jnp.dot(
                gpbuf[pl.ds(first * 2 + h, 1)][0], wsel[1], preferred_element_type=f32
            ).reshape(QB, BLK, DQ)
            if keep:
                gown[h * QB : (h + 1) * QB] = part
            else:
                gsend[h * QB : (h + 1) * QB] = part.astype(bf16)
                half = pl.ds(h * QB, QB)
                send(gsend.at[half], grecv.at[half], gs_sem.at[h], sib)

    in_part(other, False)
    in_part(c, True)
    for h in range(2):
        half = pl.ds(h * QB, QB)
        arrive(grecv.at[half], gs_sem.at[h])

    def own_sum(y_, zh_):
        b = y_ * NZ + zh_
        return gown[pl.ds(b, 1)][0] + grecv[pl.ds(b, 1)][0].astype(f32)

    for s in range(1, hops[0] + 1):
        for v in order:
            for d in range(2):
                if s <= hops[d]:
                    far = hops[d] + 1 - s
                    val = own_sum(ring(y + far * sg if d == 0 else y - far * sg, NY), v)
                    if s > 1:
                        arrive(rrecv.at[d, s - 2, v], ry_sem.at[d, s - 2, v])
                        val += rrecv[d, s - 2, pl.ds(v, 1)][0].astype(f32)
                    rsend[d, s - 1, pl.ds(v, 1)] = val.astype(bf16)[None]
                    send(
                        rsend.at[d, s - 1, v], rrecv.at[d, s - 1, v], ry_sem.at[d, s - 1, v],
                        fwd if d == 0 else bwd,
                    )
    for v in zhs + [zh]:
        val = own_sum(y, v)
        for d in range(2):
            s = hops[d] - 1
            arrive(rrecv.at[d, s, v], ry_sem.at[d, s, v])
            val += rrecv[d, s, pl.ds(v, 1)][0].astype(f32)
        if v is zh:
            zown[...] = val
        else:
            zsend[pl.ds(v, 1)] = val.astype(bf16)[None]
            send(zsend.at[v], zrecv.at[zh], rz_sem.at[zh], at(zh_=v))

    ring_end(1)
    weight_part(1, gpbuf)

    val = zown[...]
    for v in zhs:
        arrive(zrecv.at[v], rz_sem.at[v])
        val += zrecv[pl.ds(v, 1)][0].astype(f32)
    fbuf[...] = val
    for p in range(NX):
        osrc[p] = fbuf[ROWS * p : ROWS * (p + 1)].astype(bf16)
    for v in xs:
        send(osrc.at[v], obuf.at[x], ro_sem.at[x], at(x_=v))
    obuf[pl.ds(x, 1)] = osrc[pl.ds(x, 1)]

    weight_sum(0, gwo_ref)

    for v in xs:
        arrive(obuf.at[v], ro_sem.at[v])
    pieces = [obuf[p].astype(f32) for p in range(NX)]
    gin_ref[...] = jnp.concatenate(
        [pieces[p][:, k * DP : (k + 1) * DP] for k in range(NL) for p in range(NX)], axis=1
    ).astype(bf16)

    weight_sum(1, gwi_ref)

    for cp in flying:
        cp.wait_send()


def shards(tokens_in, grad_out, pre_act, w_in, w_out):
    vmem = pl.BlockSpec(memory_space=pltpu.VMEM)
    hbm = pl.BlockSpec(memory_space=pl.ANY)
    dma = pltpu.SemaphoreType.DMA
    grad_in, gwi, gwo = pl.pallas_call(
        kernel,
        out_shape=(
            jax.ShapeDtypeStruct((ROWS, WIDE), bf16),
            jax.ShapeDtypeStruct((HID, DP), bf16),
            jax.ShapeDtypeStruct((HID, DP), bf16),
        ),
        in_specs=[vmem, vmem, vmem, hbm, hbm],
        out_specs=(vmem, vmem, vmem),
        scratch_shapes=[
            pltpu.VMEM((2, NX, ROWS, DQ), bf16),
            pltpu.VMEM((2, NX, ROWS, DQ), bf16),
            pltpu.VMEM((BLK, DQ), f32),
            pltpu.VMEM((2, NBLK, BLK, DQ), bf16),
            pltpu.VMEM((2, NL, HID, WIN), bf16),
            pltpu.VMEM((2, HID, DQ), bf16),
            pltpu.VMEM((NX, QR, HID), bf16),
            pltpu.VMEM((NX, QR, HID), f32),
            pltpu.VMEM((NX, QR, HID), bf16),
            pltpu.VMEM((NX, QR, HID), bf16),
            pltpu.VMEM((QR, HID), f32),
            pltpu.VMEM((NX, QR, HID), bf16),
            pltpu.VMEM((NX, QR, HID), bf16),
            pltpu.VMEM((2, NL, HID, DP), bf16),
            pltpu.VMEM((2, NL, HID, DP), bf16),
            pltpu.VMEM((NB, BLK, DQ), f32),
            pltpu.VMEM((NB, BLK, DQ), bf16),
            pltpu.VMEM((NB, BLK, DQ), bf16),
            pltpu.VMEM((2, NY // 2, NZ, BLK, DQ), bf16),
            pltpu.VMEM((2, NY // 2, NZ, BLK, DQ), bf16),
            pltpu.VMEM((BLK, DQ), f32),
            pltpu.VMEM((NZ, BLK, DQ), bf16),
            pltpu.VMEM((NZ, BLK, DQ), bf16),
            pltpu.VMEM((BLK, DQ), f32),
            pltpu.VMEM((NX, ROWS, DQ), bf16),
            pltpu.VMEM((NX, ROWS, DQ), bf16),
            dma((160,)),
            dma((2, NX)),
            dma((NX,)),
            dma((2, NZ)),
            dma((2, 2, NY // 2, NZ)),
            dma((2, NY)),
            dma((2, NL)),
            dma((NX,)),
            dma((NX,)),
            dma((2, NL)),
            dma((2,)),
            dma((2, NY // 2, NZ)),
            dma((NZ,)),
            dma((NX,)),
        ],
        compiler_params=pltpu.CompilerParams(
            collective_id=0, has_side_effects=True, vmem_limit_bytes=48 * 1024 * 1024
        ),
        cost_estimate=pl.CostEstimate(
            flops=8 * 192 * 288 * 5120, bytes_accessed=4 * 1024 * 1024, transcendentals=0
        ),
        name="ffn_backward",
    )(grad_out, tokens_in, pre_act, w_out, w_in.T)
    return grad_in, gwi.T, gwo


def solution(mesh):
    placed = (
        P(("tokens", "mp"), None),
        P(("tokens", "mp"), None),
        P("tokens", "mp"),
        P(None, "mp"),
        P("mp", None),
    )
    return jax.shard_map(
        shards,
        mesh=mesh,
        in_specs=placed,
        out_specs=(P(("tokens", "mp"), None), P("tokens", "mp"), P("mp", "tokens")),
        check_vma=False,
    )
```

time: 610 us -> 113 us (0.19)
  the two profiles are of different devices: /device:TPU:128 before, /device:TPU:64 now
where the time goes in v1:
time: 113 us; the launch traced here: 112 us
  Pallas kernels  105 us (93%)
  local copies, waits for them, and re-layouts  6.28 us (6%)
    pallas_call x1, Pallas kernels, shards(): pl.pallas_call(kernel, out_shape=(jax.ShapeDtypeStruct((ROWS, WIDE), bf16...  105 us
    unnamed x11, local copies, waits for them, and re-layouts  6.28 us

profile of v1, /device:TPU:64, one launch (start us, length us, event | category | flops | bytes accessed | tf_op | source)
XLA Modules:
  0.0 112.2 jit_solution(12013668295646149325)
XLA Ops:
  0.6 0.0 copy-start
  0.6 1.8 %copy-done = bf16[288,5120]{1,0:T(8,128)(2,1)S(1)} copy-done((bf16[288,5120]{1,0:T(8,128)(2,1)S(1)}, bf16[288,5120]{1,0:T(8,128)(2,1)}, u32[]{:S(2)}) %copy-start) | copy-done | bytes 2949144
  2.5 0.0 copy-start.1
  2.5 0.9 copy-done.1
  3.4 0.0 copy-start.2
  3.4 0.8 copy-done.2
  4.2 0.0 copy-start.3
  4.2 0.8 copy-done.3
  4.9 105.3 %ffn_backward.1 = (bf16[4,5120]{1,0:T(4,128)(2,1)S(1)}, bf16[288,320]{1,0:T(8,128)(2,1)S(1)}, bf16[288,320]{1,0:T(8,128)(2,1)S(1)}) custom-call(bf16[4,5120]{1,0:T(4,128)(2,1)S(1)} %copy-done.2, bf16[4,5120]{1,0:T(4,128)(2,1)S(1)} %copy-done.3, bf16[192,288]{1,0:T(8,128)(2,1)S(1)} %copy-done.1, bf16[288,5120]{1,0:T(8,128)(2,1)S(1)} %copy-done, ...), custom_call_target="tpu_custom_call" | custom-call | flops 2264924160 | bytes 4194304 | tf_op jit(solution)/shard_map/ffn_backward/pallas_call | solution.py:359
  110.2 0.6 copy.11
  110.8 0.7 copy.12
  111.5 0.7 copy.13
Async XLA Ops:
  0.6 1.8 %copy-start = (bf16[288,5120]{1,0:T(8,128)(2,1)S(1)}, bf16[288,5120]{1,0:T(8,128)(2,1)}, u32[]{:S(2)}) copy-start(bf16[288,5120]{1,0:T(8,128)(2,1)} %wo_ref.1) | copy-start | bytes 8847364
  2.5 0.9 copy-start.1
  3.4 0.8 copy-start.2
  4.2 0.8 copy-start.3

commit v2 on v1

v2 whole, which is shorter than its diff:
```python
import math

import jax
import jax.numpy as jnp
from jax import lax
from jax.experimental import pallas as pl
from jax.experimental.pallas import tpu as pltpu
from jax.sharding import PartitionSpec as P

root_two_pi = math.sqrt(2.0 / math.pi)
cubic = 0.044715

NY, NZ, NC = 8, 3, 2
NL, NX = 4, 4
ROWS = 4
BLK = ROWS * NX
NB = NY * NZ
NBLK = NC * NB
QR = NBLK * ROWS
GRP = NBLK // 4
GR = GRP * ROWS
NW = 4
WIDE = 5120
HID = 288
DQ = WIDE // NX
DP = DQ // NL
WIN = 384
MESH = pl.DeviceIdType.MESH
f32 = jnp.float32
bf16 = jnp.bfloat16


def gelu_value(pre):
    inner = root_two_pi * (pre + cubic * pre * pre * pre)
    return 0.5 * pre * (1.0 + jnp.tanh(inner))


def gelu_slope(pre):
    tanh_val = jnp.tanh(root_two_pi * (pre + cubic * pre * pre * pre))
    return 0.5 * (1.0 + tanh_val) + 0.5 * pre * (1.0 - tanh_val * tanh_val) * root_two_pi * (
        1.0 + 3.0 * cubic * pre * pre
    )


def kernel(
    go_ref, ti_ref, pre_ref, wo_ref, wi_ref,
    gin_ref, gwi_ref, gwo_ref,
    rows_in, xsrc, xbuf, mbuf, gbuf, sel, prebuf, wo, wi, slope, act, gpbuf, cgo, cti, gw,
    wchunk, wpair, wfar, wlast, gflat, gfold, grecv, rsend, rrecv, zown, zsend, zrecv,
    send_sem, in_sem, w_sem, x_sem, zg_sem, y_sem, sib_sem, act_sem, ag_sem, gw_sem, gwl_sem, gwsib_sem,
    wp_sem, wl_sem, gs_sem, ry_sem, rz_sem,
):
    m = lax.axis_index("mp")
    t = lax.axis_index("tokens")
    c = lax.rem(m, NC)
    zh = lax.rem(m // NC, NZ)
    y = m // (NC * NZ)
    x = lax.rem(t, NX)
    zl = t // NX
    sg = 1 - 2 * c

    def at(y_=None, zh_=None, c_=None, zl_=None, x_=None):
        y_ = y if y_ is None else y_
        zh_ = zh if zh_ is None else zh_
        c_ = c if c_ is None else c_
        zl_ = zl if zl_ is None else zl_
        x_ = x if x_ is None else x_
        return {"mp": (y_ * NZ + zh_) * NC + c_, "tokens": zl_ * NX + x_}

    def ring(v, n):
        return lax.rem(v + n, n)

    other = 1 - c
    xs = [lax.rem(x + d, NX) for d in range(1, NX)]
    zhs = [lax.rem(zh + d, NZ) for d in range(1, NZ)]
    near = zl + 1 - 2 * lax.rem(zl, 2)
    far_zl = lax.rem(zl + 2, NL)
    far_near = lax.rem(near + 2, NL)
    fwd = at(y_=ring(y + sg, NY))
    bwd = at(y_=ring(y - sg, NY))
    sib = at(c_=other)
    flying = []

    def send(src, dst, sem, dev):
        cp = pltpu.make_async_remote_copy(
            src_ref=src, dst_ref=dst, send_sem=send_sem.at[len(flying)], recv_sem=sem,
            device_id=dev, device_id_type=MESH,
        )
        cp.start()
        flying.append(cp)

    def arrive(dst, sem):
        pltpu.make_async_remote_copy(
            src_ref=dst, dst_ref=dst, send_sem=send_sem.at[0], recv_sem=sem,
            device_id=sib, device_id_type=MESH,
        ).wait_recv()

    first = [
        pltpu.make_async_copy(go_ref, rows_in.at[0], in_sem.at[0]),
        pltpu.make_async_copy(ti_ref, rows_in.at[1], in_sem.at[1]),
        pltpu.make_async_copy(pre_ref, prebuf, in_sem.at[2]),
    ]
    for cp in first:
        cp.start()

    barrier = pltpu.get_barrier_semaphore()
    peers = (
        [at(x_=v) for v in xs] + [at(zh_=v) for v in zhs] + [at(zl_=near), at(zl_=far_zl)]
        + [fwd, bwd, sib]
    )
    for dev in peers:
        pl.semaphore_signal(barrier, inc=1, device_id=dev, device_id_type=MESH)

    loads = [
        pltpu.make_async_copy(wo_ref, wo, w_sem.at[0]),
        pltpu.make_async_copy(wi_ref, wi, w_sem.at[1]),
    ]
    for cp in loads:
        cp.start()

    def block(y_, zh_, c_):
        return c_ * NB + y_ * NZ + zh_

    first[0].wait()
    v = rows_in[0].astype(f32)
    for n in range(NW):
        mbuf[ROWS * n : ROWS * (n + 1)] = v[:, n * DQ : (n + 1) * DQ]
    gbuf[0, pl.ds(block(y, zh, c), 1)] = mbuf[...].astype(bf16)[None]
    first[1].wait()
    v = rows_in[1].astype(f32)
    for p in range(NX):
        xsrc[p] = jnp.concatenate(
            [v[:, k * DQ + p * DP : k * DQ + (p + 1) * DP] for k in range(NL)], axis=1
        ).astype(bf16)

    pl.semaphore_wait(barrier, len(peers))

    def spread(a):
        mine = gbuf.at[a, block(y, zh, c)]
        for v in zhs:
            send(mine, mine, zg_sem.at[a, zh], at(zh_=v))

    def hop(a, d, s, y_, zh_):
        ref = gbuf.at[a, block(y_, zh_, c)]
        send(ref, ref, y_sem.at[a, d, s, zh_], fwd if d == 0 else bwd)

    def to_sib(a, y_):
        ref = gbuf.at[a, pl.ds(block(y_, 0, c), NZ)]
        send(ref, ref, sib_sem.at[a, y_], sib)

    order = [zh] + zhs
    hops = (NY // 2, NY // 2 - 1)

    def ring_first(a, i):
        v = order[i]
        if i:
            ref = gbuf.at[a, block(y, v, c)]
            arrive(ref, zg_sem.at[a, v])
        hop(a, 0, 0, y, v)
        hop(a, 1, 0, y, v)
        if i == NZ - 1:
            to_sib(a, y)

    def ring_step(a, s):
        for i in range(NZ):
            v = order[i]
            for d in range(2):
                if s <= hops[d]:
                    y_ = ring(y - s * sg if d == 0 else y + s * sg, NY)
                    arrive(gbuf.at[a, block(y_, v, c)], y_sem.at[a, d, s - 1, v])
                    if s < hops[d]:
                        hop(a, d, s, y_, v)
                    if i == NZ - 1:
                        to_sib(a, y_)

    spread(0)
    ring_first(0, 0)
    for v in xs:
        send(xsrc.at[v], xbuf.at[x], x_sem.at[x], at(x_=v))
    xbuf[pl.ds(x, 1)] = xsrc[pl.ds(x, 1)]

    pairs = [(y, ring(y + 4, NY))] + [(ring(y + g, NY), ring(y - g, NY)) for g in range(1, 4)]
    i = lax.broadcasted_iota(jnp.int32, (QR, QR), 0)
    j = lax.broadcasted_iota(jnp.int32, (QR, QR), 1)

    n = (i >= GR).astype(jnp.int32) + (i >= 2 * GR).astype(jnp.int32) + (i >= 3 * GR).astype(jnp.int32)
    sel[...] = jnp.where(((i >> 2) - GRP * n) * BLK + n * ROWS + (i & 3) == j, 1.0, 0.0).astype(bf16)

    first[2].wait()
    q = (i * 43691) >> 19
    rest = i - 12 * q
    g = q >> 2
    ahead = jnp.where((q & 2) == 0, g, jnp.where(g == 0, 4, NY - g))
    src = ((y + ahead) & (NY - 1)) * (NZ * NC * ROWS) + (rest >> 2) * (NC * ROWS) + (q & 1) * ROWS + (rest & 3)
    hot = jnp.where(src == j, 1.0, 0.0).astype(bf16)
    pre = jnp.dot(hot, prebuf[...], preferred_element_type=f32)
    slope[...] = gelu_slope(pre)
    act[pl.ds(x, 1)] = gelu_value(pre).astype(bf16)[None]
    for v in xs:
        send(act.at[x], act.at[x], act_sem.at[x], at(x_=v))

    ring_first(0, 1)
    ring_first(0, 2)

    for v in xs:
        arrive(xbuf.at[v], x_sem.at[v])
    for p in range(NX):
        mbuf[ROWS * p : ROWS * (p + 1)] = xbuf[p].astype(f32)
    gbuf[1, pl.ds(block(y, zh, c), 1)] = mbuf[...].astype(bf16)[None]
    spread(1)

    def group(a, g):
        for y_ in pairs[g]:
            arrive(gbuf.at[a, pl.ds(block(y_, 0, other), NZ)], sib_sem.at[a, y_])
        rows = [gbuf[a, pl.ds(block(y_, 0, c_), NZ)] for y_ in pairs[g] for c_ in range(NC)]
        return jnp.dot(
            sel[...], jnp.concatenate(rows, axis=0).reshape(QR, DQ), preferred_element_type=f32
        ).astype(bf16)

    def window(v, n):
        low = pl.multiple_of(((v * DP) // 128) * 128, 128)
        return pl.ds(pl.multiple_of(low + n * DQ, 128), WIN)

    def out_group(g):
        part = group(0, g)
        rows = slice(g * GR, (g + 1) * GR)
        for n in range(NW):
            cgo[rows, n * DQ : (n + 1) * DQ] = part[n * GR : (n + 1) * GR]
        for v in xs:
            for k in range(2):
                n = 2 * c + k
                send(
                    cgo.at[rows, window(v, n)], gw.at[n, x, rows], gw_sem.at[x, g, k], at(x_=v)
                )

    def pass_on(g):
        rows = slice(g * GR, (g + 1) * GR)
        for v in xs:
            for k in range(2):
                arrive(gw.at[2 * c + k, v, rows], gw_sem.at[v, g, k])
            mine = gw.at[pl.ds(2 * c, 2), v, rows]
            send(mine, mine, gwsib_sem.at[v, g], sib)

    ring_step(0, 1)
    ring_step(0, 2)
    out_group(1)
    ring_step(0, 3)
    out_group(2)
    ring_step(0, 4)
    for i in range(NZ):
        ring_first(1, i)
    out_group(3)
    out_group(0)
    pass_on(1)
    pass_on(2)
    own = [
        pltpu.make_async_copy(cgo.at[:, window(x, n)], gw.at[n, x], gwl_sem.at[n]) for n in range(NW)
    ]
    for cp in own:
        cp.start()

    for cp in loads:
        cp.wait()
    grad_act = lax.dot_general(
        cgo[...], wo[...], (((1,), (1,)), ((), ())), preferred_element_type=f32
    )
    gpbuf[pl.ds(x, 1)] = (grad_act * slope[...]).astype(bf16)[None]
    for v in xs:
        send(gpbuf.at[x], gpbuf.at[x], ag_sem.at[x], at(x_=v))

    ring_step(1, 1)

    grad_pre = gpbuf[pl.ds(x, 1)][0]
    for n in range(NW):
        part = jnp.dot(grad_pre, wi[:, n * DQ : (n + 1) * DQ], preferred_element_type=f32)
        gflat[n] = part.astype(bf16)
    for g in range(4):
        rows = gflat[:, g * GR : (g + 1) * GR, :].reshape(QR, DQ)
        part = lax.dot_general(
            sel[...], rows, (((0,), (0,)), ((), ())), preferred_element_type=f32
        ).astype(bf16).reshape(GRP, BLK, DQ)
        k = 0
        for y_ in pairs[g]:
            for c_ in range(NC):
                gfold[c_, pl.ds(y_ * NZ, NZ)] = part[k : k + NZ]
                k += NZ
    for h in range(2):
        some = pl.ds(h * (NB // 2), NB // 2)
        send(gfold.at[other, some], grecv.at[some], gs_sem.at[h], sib)

    ring_step(1, 2)
    pass_on(3)
    pass_on(0)

    for h in range(2):
        some = pl.ds(h * (NB // 2), NB // 2)
        arrive(grecv.at[some], gs_sem.at[h])

    def own_sum(y_, zh_):
        b = y_ * NZ + zh_
        return gfold[c, pl.ds(b, 1)][0].astype(f32) + grecv[pl.ds(b, 1)][0].astype(f32)

    def sum_step(s):
        for v in order:
            for d in range(2):
                if s <= hops[d]:
                    far = hops[d] + 1 - s
                    val = own_sum(ring(y + far * sg if d == 0 else y - far * sg, NY), v)
                    if s > 1:
                        arrive(rrecv.at[d, s - 2, v], ry_sem.at[d, s - 2, v])
                        val += rrecv[d, s - 2, pl.ds(v, 1)][0].astype(f32)
                    rsend[d, s - 1, pl.ds(v, 1)] = val.astype(bf16)[None]
                    send(
                        rsend.at[d, s - 1, v], rrecv.at[d, s - 1, v], ry_sem.at[d, s - 1, v],
                        fwd if d == 0 else bwd,
                    )

    scale_back = 1.0 / math.sqrt(NL * NX * NC * NB * ROWS)
    odd = lax.rem(x, 2)

    def weight_part(lhs, right):
        return (
            lax.dot_general(lhs, right, (((0,), (0,)), ((), ())), preferred_element_type=f32)
            * scale_back
        )

    def put_chunk(a, k, piece):
        wchunk[a, k] = jnp.concatenate([piece[: HID // 2], piece[HID // 2 :]], axis=1).astype(bf16)

    def weight_pair(a):
        dev = at(zl_=near)
        send(wchunk.at[a, far_near], wpair.at[a, 1], wp_sem.at[a, 1], dev)
        send(wchunk.at[a, near], wpair.at[a, 0], wp_sem.at[a, 0], dev)

    def weight_far(a):
        arrive(wpair.at[a, 1], wp_sem.at[a, 1])
        val = wchunk[a, pl.ds(far_zl, 1)][0].astype(f32) + wpair[a, 1].astype(f32)
        wfar[a] = val.astype(bf16)
        send(wfar.at[a], wlast.at[a], wl_sem.at[a], at(zl_=far_zl))

    def weight_sum(a, out):
        arrive(wpair.at[a, 0], wp_sem.at[a, 0])
        arrive(wlast.at[a], wl_sem.at[a])
        val = wchunk[a, pl.ds(zl, 1)][0].astype(f32)
        val = (val + wpair[a, 0].astype(f32) + wlast[a].astype(f32)).astype(bf16)
        out[: HID // 2] = val[:, :DP]
        out[HID // 2 :] = val[:, DP:]

    sum_step(1)
    ring_step(1, 3)

    for cp in own:
        cp.wait()
    for v in xs:
        arrive(act.at[v], act_sem.at[v])
        for g in range(4):
            arrive(gw.at[pl.ds(2 * other, 2), v, slice(g * GR, (g + 1) * GR)], gwsib_sem.at[v, g])
    left = act[...].reshape(NX * QR, HID)
    for n in range(NW):
        part = weight_part(left, gw[n].reshape(NX * QR, WIN))
        turned = pltpu.roll(part, WIN - DP % 128, 1)
        put_chunk(0, n, jnp.where(odd == 1, turned, part)[:, :DP])
    weight_pair(0)

    sum_step(2)
    ring_step(1, 4)
    for g in (1, 2, 3, 0):
        part = group(1, g)
        for p in range(NX):
            cti[p * QR + g * GR : p * QR + (g + 1) * GR] = part[p * GR : (p + 1) * GR]
        if g == 2:
            sum_step(3)

    for v in xs:
        arrive(gpbuf.at[v], ag_sem.at[v])
    left = gpbuf[...].reshape(NX * QR, HID)
    for h in range(2):
        part = weight_part(left, cti[:, 2 * h * DP : 2 * (h + 1) * DP])
        for k in range(2):
            put_chunk(1, 2 * h + k, part[:, k * DP : (k + 1) * DP])
        if h == 0:
            sum_step(4)
    weight_pair(1)
    weight_far(0)

    for i, v in enumerate(zhs + [zh]):
        val = own_sum(y, v)
        for d in range(2):
            s = hops[d] - 1
            arrive(rrecv.at[d, s, v], ry_sem.at[d, s, v])
            val += rrecv[d, s, pl.ds(v, 1)][0].astype(f32)
        if i == NZ - 1:
            zown[...] = val
        else:
            zsend[pl.ds(v, 1)] = val.astype(bf16)[None]
            send(zsend.at[v], zrecv.at[zh], rz_sem.at[zh], at(zh_=v))

    weight_far(1)

    val = zown[...]
    for v in zhs:
        arrive(zrecv.at[v], rz_sem.at[v])
        val += zrecv[pl.ds(v, 1)][0].astype(f32)
    for n in range(NW):
        gin_ref[:, n * DQ : (n + 1) * DQ] = val[ROWS * n : ROWS * (n + 1)].astype(bf16)

    weight_sum(0, gwo_ref)
    weight_sum(1, gwi_ref)

    for cp in flying:
        cp.wait_send()


def deliver(a_ref, b_ref, d_ref, a_out, b_out, d_out):
    a_out[...] = a_ref[...]
    b_out[...] = b_ref[...]
    d_out[...] = d_ref[...]


def shards(tokens_in, grad_out, pre_act, w_in, w_out):
    vmem = pl.BlockSpec(memory_space=pltpu.VMEM)
    hbm = pl.BlockSpec(memory_space=pltpu.HBM)
    dma = pltpu.SemaphoreType.DMA
    shapes = (
        jax.ShapeDtypeStruct((ROWS, WIDE), bf16),
        jax.ShapeDtypeStruct((HID, DP), bf16),
        jax.ShapeDtypeStruct((HID, DP), bf16),
    )
    outs = pl.pallas_call(
        kernel,
        out_shape=shapes,
        in_specs=[hbm] * 5,
        out_specs=(vmem, vmem, vmem),
        scratch_shapes=[
            pltpu.VMEM((2, ROWS, WIDE), bf16),
            pltpu.VMEM((NX, ROWS, DQ), bf16),
            pltpu.VMEM((NX, ROWS, DQ), bf16),
            pltpu.VMEM((BLK, DQ), f32),
            pltpu.VMEM((2, NBLK, BLK, DQ), bf16),
            pltpu.VMEM((QR, QR), bf16),
            pltpu.VMEM((QR, HID), bf16),
            pltpu.VMEM((HID, WIDE), bf16),
            pltpu.VMEM((HID, WIDE), bf16),
            pltpu.VMEM((QR, HID), f32),
            pltpu.VMEM((NX, QR, HID), bf16),
            pltpu.VMEM((NX, QR, HID), bf16),
            pltpu.VMEM((QR, WIDE), bf16),
            pltpu.VMEM((NX * QR, DQ), bf16),
            pltpu.VMEM((NW, NX, QR, WIN), bf16),
            pltpu.VMEM((2, NL, HID // 2, 2 * DP), bf16),
            pltpu.VMEM((2, 2, HID // 2, 2 * DP), bf16),
            pltpu.VMEM((2, HID // 2, 2 * DP), bf16),
            pltpu.VMEM((2, HID // 2, 2 * DP), bf16),
            pltpu.VMEM((NW, QR, DQ), bf16),
            pltpu.VMEM((NC, NB, BLK, DQ), bf16),
            pltpu.VMEM((NB, BLK, DQ), bf16),
            pltpu.VMEM((2, NY // 2, NZ, BLK, DQ), bf16),
            pltpu.VMEM((2, NY // 2, NZ, BLK, DQ), bf16),
            pltpu.VMEM((BLK, DQ), f32),
            pltpu.VMEM((NZ, BLK, DQ), bf16),
            pltpu.VMEM((NZ, BLK, DQ), bf16),
            dma((200,)),
            dma((3,)),
            dma((2,)),
            dma((NX,)),
            dma((2, NZ)),
            dma((2, 2, NY // 2, NZ)),
            dma((2, NY)),
            dma((NX,)),
            dma((NX,)),
            dma((NX, 4, 2)),
            dma((NW,)),
            dma((NX, 4)),
            dma((2, 2)),
            dma((2,)),
            dma((2,)),
            dma((2, NY // 2, NZ)),
            dma((NZ,)),
        ],
        compiler_params=pltpu.CompilerParams(
            collective_id=0, has_side_effects=True, vmem_limit_bytes=60 * 1024 * 1024
        ),
        cost_estimate=pl.CostEstimate(
            flops=8 * 192 * 288 * 5120, bytes_accessed=4 * 1024 * 1024, transcendentals=0
        ),
        name="ffn_backward",
    )(grad_out, tokens_in, pre_act, w_out, w_in.T)
    grad_in, gwi, gwo = pl.pallas_call(
        deliver,
        out_shape=shapes,
        in_specs=[vmem] * 3,
        out_specs=(vmem,) * 3,
        compiler_params=pltpu.CompilerParams(vmem_limit_bytes=60 * 1024 * 1024),
        name="deliver",
    )(*outs)
    return grad_in, gwi.T, gwo


def solution(mesh):
    placed = (
        P(("tokens", "mp"), None),
        P(("tokens", "mp"), None),
        P("tokens", "mp"),
        P(None, "mp"),
        P("mp", None),
    )
    return jax.shard_map(
        shards,
        mesh=mesh,
        in_specs=placed,
        out_specs=(P(("tokens", "mp"), None), P("tokens", "mp"), P("mp", "tokens")),
        check_vma=False,
    )
```

time: 113 us -> 91 us (0.81)
  the two profiles are of different devices: /device:TPU:64 before, /device:TPU:6 now
where the time goes in v2:
time: 91 us; the launch traced here: 89.3 us
  Pallas kernels  88.7 us (97%)
    pallas_call x1, Pallas kernels, shards(): pl.pallas_call(kernel, out_shape=shapes, in_specs=[hbm] * 5, out_specs=(v...  86.8 us
    pallas_call x1, Pallas kernels, shards(): pl.pallas_call(deliver, out_shape=shapes, in_specs=[vmem] * 3, out_specs=...  1.86 us

profile of v2, /device:TPU:6, one launch (start us, length us, event | category | flops | bytes accessed | tf_op | source)
XLA Modules:
  0.0 89.3 jit_solution(10524675384497600925)
XLA Ops:
  0.6 86.8 %ffn_backward.1 = (bf16[4,5120]{1,0:T(4,128)(2,1)}, bf16[288,320]{1,0:T(8,128)(2,1)}, bf16[288,320]{1,0:T(8,128)(2,1)}) custom-call(bf16[4,5120]{1,0:T(4,128)(2,1)} %go_ref.1, bf16[4,5120]{1,0:T(4,128)(2,1)} %ti_ref.1, bf16[192,288]{1,0:T(8,128)(2,1)} %pre_ref.1, bf16[288,5120]{1,0:T(8,128)(2,1)} %wo_ref.1, bf16[288,5120]{1,0:T(8,128)(2,1)} %bitcast.2), custom_call_target="tpu_custom_call" | custom-call | flops 2264924160 | bytes 4194304 | tf_op jit(solution)/shard_map/ffn_backward/pallas_call | solution.py:429
  87.5 1.9 %deliver.1 = (bf16[4,5120]{1,0:T(4,128)(2,1)}, bf16[288,320]{1,0:T(8,128)(2,1)}, bf16[288,320]{1,0:T(8,128)(2,1)}) custom-call(bf16[4,5120]{1,0:T(4,128)(2,1)} %get-tuple-element.9.a_ref, bf16[288,320]{1,0:T(8,128)(2,1)} %get-tuple-element.10.b_ref, bf16[288,320]{1,0:T(8,128)(2,1)} %get-tuple-element.11.d_ref), custom_call_target="tpu_custom_call" | custom-call | tf_op jit(solution)/shard_map/deliver/pallas_call | solution.py:488

commit v3 on v2

--- a/solution.py
+++ b/solution.py
@@ -24,7 +24,8 @@
 HID = 288
 DQ = WIDE // NX
 DP = DQ // NL
-WIN = 384
+NH = NZ * NL
+HQ = DQ // NC
 MESH = pl.DeviceIdType.MESH
 f32 = jnp.float32
 bf16 = jnp.bfloat16
@@ -46,9 +47,9 @@
     go_ref, ti_ref, pre_ref, wo_ref, wi_ref,
     gin_ref, gwi_ref, gwo_ref,
     rows_in, xsrc, xbuf, mbuf, gbuf, sel, prebuf, wo, wi, slope, act, gpbuf, cgo, cti, gw,
-    wchunk, wpair, wfar, wlast, gflat, gfold, grecv, rsend, rrecv, zown, zsend, zrecv,
+    wchunk, wpair, wfar, wlast, wx, gflat, gfold, grecv, rsend, rrecv, zown, zsend, zrecv,
     send_sem, in_sem, w_sem, x_sem, zg_sem, y_sem, sib_sem, act_sem, ag_sem, gw_sem, gwl_sem, gwsib_sem,
-    wp_sem, wl_sem, gs_sem, ry_sem, rz_sem,
+    wp_sem, wl_sem, wx_sem, gs_sem, ry_sem, rz_sem,
 ):
     m = lax.axis_index("mp")
     t = lax.axis_index("tokens")
@@ -73,6 +74,13 @@
     other = 1 - c
     xs = [lax.rem(x + d, NX) for d in range(1, NX)]
     zhs = [lax.rem(zh + d, NZ) for d in range(1, NZ)]
+    zls = [lax.rem(zl + d, NL) for d in range(1, NL)]
+    z = zh * NL + zl
+
+    def along(d):
+        z_ = lax.rem(z + d + NH, NH)
+        return at(zh_=z_ // NL, zl_=lax.rem(z_, NL))
+
     near = zl + 1 - 2 * lax.rem(zl, 2)
     far_zl = lax.rem(zl + 2, NL)
     far_near = lax.rem(near + 2, NL)
@@ -105,7 +113,7 @@
 
     barrier = pltpu.get_barrier_semaphore()
     peers = (
-        [at(x_=v) for v in xs] + [at(zh_=v) for v in zhs] + [at(zl_=near), at(zl_=far_zl)]
+        [at(x_=v) for v in xs] + [along(d) for d in (1, 2, 3, 4, -1, -2, -3, -4)]
         + [fwd, bwd, sib]
     )
     for dev in peers:
@@ -195,9 +203,7 @@
     hot = jnp.where(src == j, 1.0, 0.0).astype(bf16)
     pre = jnp.dot(hot, prebuf[...], preferred_element_type=f32)
     slope[...] = gelu_slope(pre)
-    act[pl.ds(x, 1)] = gelu_value(pre).astype(bf16)[None]
-    for v in xs:
-        send(act.at[x], act.at[x], act_sem.at[x], at(x_=v))
+    act[pl.ds(zl, 1)] = gelu_value(pre).astype(bf16)[None]
 
     ring_first(0, 1)
     ring_first(0, 2)
@@ -208,6 +214,8 @@
         mbuf[ROWS * p : ROWS * (p + 1)] = xbuf[p].astype(f32)
     gbuf[1, pl.ds(block(y, zh, c), 1)] = mbuf[...].astype(bf16)[None]
     spread(1)
+    for v in zls:
+        send(act.at[zl], act.at[zl], act_sem.at[zl], at(zl_=v))
 
     def group(a, g):
         for y_ in pairs[g]:
@@ -217,47 +225,41 @@
             sel[...], jnp.concatenate(rows, axis=0).reshape(QR, DQ), preferred_element_type=f32
         ).astype(bf16)
 
-    def window(v, n):
-        low = pl.multiple_of(((v * DP) // 128) * 128, 128)
-        return pl.ds(pl.multiple_of(low + n * DQ, 128), WIN)
-
     def out_group(g):
         part = group(0, g)
         rows = slice(g * GR, (g + 1) * GR)
         for n in range(NW):
             cgo[rows, n * DQ : (n + 1) * DQ] = part[n * GR : (n + 1) * GR]
-        for v in xs:
-            for k in range(2):
-                n = 2 * c + k
-                send(
-                    cgo.at[rows, window(v, n)], gw.at[n, x, rows], gw_sem.at[x, g, k], at(x_=v)
-                )
+
+    def out_send(g):
+        rows = slice(g * GR, (g + 1) * GR)
+        for v, d in zip(zls, (1, 2 * sg, -1)):
+            send(
+                cgo.at[rows, cols(v * DQ + c * HQ)], gw.at[zl, rows, cols(c * HQ)], gw_sem.at[zl, g], along(d)
+            )
+
+    def cols(low):
+        return pl.ds(pl.multiple_of(low, 128), HQ)
 
     def pass_on(g):
         rows = slice(g * GR, (g + 1) * GR)
-        for v in xs:
-            for k in range(2):
-                arrive(gw.at[2 * c + k, v, rows], gw_sem.at[v, g, k])
-            mine = gw.at[pl.ds(2 * c, 2), v, rows]
+        for v in zls:
+            mine = gw.at[v, rows, cols(c * HQ)]
+            arrive(mine, gw_sem.at[v, g])
             send(mine, mine, gwsib_sem.at[v, g], sib)
 
     ring_step(0, 1)
     ring_step(0, 2)
     out_group(1)
+    out_send(1)
     ring_step(0, 3)
     out_group(2)
+    out_send(2)
     ring_step(0, 4)
     for i in range(NZ):
         ring_first(1, i)
     out_group(3)
     out_group(0)
-    pass_on(1)
-    pass_on(2)
-    own = [
-        pltpu.make_async_copy(cgo.at[:, window(x, n)], gw.at[n, x], gwl_sem.at[n]) for n in range(NW)
-    ]
-    for cp in own:
-        cp.start()
 
     for cp in loads:
         cp.wait()
@@ -289,8 +291,12 @@
         send(gfold.at[other, some], grecv.at[some], gs_sem.at[h], sib)
 
     ring_step(1, 2)
-    pass_on(3)
-    pass_on(0)
+    out_send(3)
+    out_send(0)
+    own = pltpu.make_async_copy(
+        cgo.at[:, pl.ds(pl.multiple_of(zl * DQ, 128), DQ)], gw.at[zl], gwl_sem.at[0]
+    )
+    own.start()
 
     for h in range(2):
         some = pl.ds(h * (NB // 2), NB // 2)
@@ -316,72 +322,70 @@
                     )
 
     scale_back = 1.0 / math.sqrt(NL * NX * NC * NB * ROWS)
-    odd = lax.rem(x, 2)
-
-    def weight_part(lhs, right):
-        return (
-            lax.dot_general(lhs, right, (((0,), (0,)), ((), ())), preferred_element_type=f32)
-            * scale_back
-        )
+
+    def weight_parts(a, lhs, right):
+        for h in range(2):
+            some = slice(2 * h * DP, 2 * (h + 1) * DP)
+            rows = right[..., some].reshape(NX * QR, 2 * DP)
+            part = scale_back * lax.dot_general(
+                lhs, rows, (((0,), (0,)), ((), ())), preferred_element_type=f32
+            )
+            for k in range(2):
+                put_chunk(a, 2 * h + k, part[:, k * DP : (k + 1) * DP])
 
     def put_chunk(a, k, piece):
         wchunk[a, k] = jnp.concatenate([piece[: HID // 2], piece[HID // 2 :]], axis=1).astype(bf16)
 
     def weight_pair(a):
         dev = at(zl_=near)
-        send(wchunk.at[a, far_near], wpair.at[a, 1], wp_sem.at[a, 1], dev)
-        send(wchunk.at[a, near], wpair.at[a, 0], wp_sem.at[a, 0], dev)
+        send(wchunk.at[a, far_near], wpair.at[1], wp_sem.at[1], dev)
+        send(wchunk.at[a, near], wpair.at[0], wp_sem.at[0], dev)
 
     def weight_far(a):
-        arrive(wpair.at[a, 1], wp_sem.at[a, 1])
-        val = wchunk[a, pl.ds(far_zl, 1)][0].astype(f32) + wpair[a, 1].astype(f32)
-        wfar[a] = val.astype(bf16)
-        send(wfar.at[a], wlast.at[a], wl_sem.at[a], at(zl_=far_zl))
-
-    def weight_sum(a, out):
-        arrive(wpair.at[a, 0], wp_sem.at[a, 0])
-        arrive(wlast.at[a], wl_sem.at[a])
-        val = wchunk[a, pl.ds(zl, 1)][0].astype(f32)
-        val = (val + wpair[a, 0].astype(f32) + wlast[a].astype(f32)).astype(bf16)
-        out[: HID // 2] = val[:, :DP]
-        out[HID // 2 :] = val[:, DP:]
-
-    sum_step(1)
-    ring_step(1, 3)
-
-    for cp in own:
-        cp.wait()
-    for v in xs:
-        arrive(act.at[v], act_sem.at[v])
-        for g in range(4):
-            arrive(gw.at[pl.ds(2 * other, 2), v, slice(g * GR, (g + 1) * GR)], gwsib_sem.at[v, g])
-    left = act[...].reshape(NX * QR, HID)
-    for n in range(NW):
-        part = weight_part(left, gw[n].reshape(NX * QR, WIN))
-        turned = pltpu.roll(part, WIN - DP % 128, 1)
-        put_chunk(0, n, jnp.where(odd == 1, turned, part)[:, :DP])
-    weight_pair(0)
-
-    sum_step(2)
-    ring_step(1, 4)
-    for g in (1, 2, 3, 0):
+        arrive(wpair.at[1], wp_sem.at[1])
+        val = wchunk[a, pl.ds(far_zl, 1)][0].astype(f32) + wpair[1].astype(f32)
+        wfar[...] = val.astype(bf16)
+        send(wfar, wlast, wl_sem.at[0], at(zl_=far_zl))
+
+    def put_sum(val, out):
+        out[: HID // 2] = val[:, :DP].astype(bf16)
+        out[HID // 2 :] = val[:, DP:].astype(bf16)
+
+    def in_group(g):
         part = group(1, g)
         for p in range(NX):
             cti[p * QR + g * GR : p * QR + (g + 1) * GR] = part[p * GR : (p + 1) * GR]
-        if g == 2:
-            sum_step(3)
+
+    sum_step(1)
+    ring_step(1, 3)
+    in_group(1)
+    sum_step(2)
+    in_group(2)
+    ring_step(1, 4)
+    sum_step(3)
+    in_group(3)
+    in_group(0)
 
     for v in xs:
         arrive(gpbuf.at[v], ag_sem.at[v])
-    left = gpbuf[...].reshape(NX * QR, HID)
-    for h in range(2):
-        part = weight_part(left, cti[:, 2 * h * DP : 2 * (h + 1) * DP])
-        for k in range(2):
-            put_chunk(1, 2 * h + k, part[:, k * DP : (k + 1) * DP])
-        if h == 0:
-            sum_step(4)
+    weight_parts(1, gpbuf[...].reshape(NX * QR, HID), cti)
     weight_pair(1)
-    weight_far(0)
+    pass_on(1)
+    pass_on(2)
+    sum_step(4)
+    pass_on(3)
+    pass_on(0)
+
+    own.wait()
+    for v in zls:
+        arrive(act.at[v], act_sem.at[v])
+        for g in range(4):
+            arrive(gw.at[v, slice(g * GR, (g + 1) * GR), cols(other * HQ)], gwsib_sem.at[v, g])
+    weight_parts(0, act[...].reshape(NX * QR, HID), gw)
+    for v in xs:
+        send(wchunk.at[0, v], wx.at[x], wx_sem.at[x], at(x_=v))
+
+    weight_far(1)
 
     for i, v in enumerate(zhs + [zh]):
         val = own_sum(y, v)
@@ -395,8 +399,6 @@
             zsend[pl.ds(v, 1)] = val.astype(bf16)[None]
             send(zsend.at[v], zrecv.at[zh], rz_sem.at[zh], at(zh_=v))
 
-    weight_far(1)
-
     val = zown[...]
     for v in zhs:
         arrive(zrecv.at[v], rz_sem.at[v])
@@ -404,8 +406,16 @@
     for n in range(NW):
         gin_ref[:, n * DQ : (n + 1) * DQ] = val[ROWS * n : ROWS * (n + 1)].astype(bf16)
 
-    weight_sum(0, gwo_ref)
-    weight_sum(1, gwi_ref)
+    val = wchunk[0, pl.ds(x, 1)][0].astype(f32)
+    for v in xs:
+        arrive(wx.at[v], wx_sem.at[v])
+        val += wx[pl.ds(v, 1)][0].astype(f32)
+    put_sum(val, gwo_ref)
+
+    arrive(wpair.at[0], wp_sem.at[0])
+    val = wchunk[1, pl.ds(zl, 1)][0].astype(f32) + wpair[0].astype(f32)
+    arrive(wlast, wl_sem.at[0])
+    put_sum(val + wlast[...].astype(f32), gwi_ref)
 
     for cp in flying:
         cp.wait_send()
@@ -446,11 +456,12 @@
             pltpu.VMEM((NX, QR, HID), bf16),
             pltpu.VMEM((QR, WIDE), bf16),
             pltpu.VMEM((NX * QR, DQ), bf16),
-            pltpu.VMEM((NW, NX, QR, WIN), bf16),
+            pltpu.VMEM((NL, QR, DQ), bf16),
             pltpu.VMEM((2, NL, HID // 2, 2 * DP), bf16),
-            pltpu.VMEM((2, 2, HID // 2, 2 * DP), bf16),
             pltpu.VMEM((2, HID // 2, 2 * DP), bf16),
-            pltpu.VMEM((2, HID // 2, 2 * DP), bf16),
+            pltpu.VMEM((HID // 2, 2 * DP), bf16),
+            pltpu.VMEM((HID // 2, 2 * DP), bf16),
+            pltpu.VMEM((NX, HID // 2, 2 * DP), bf16),
             pltpu.VMEM((NW, QR, DQ), bf16),
             pltpu.VMEM((NC, NB, BLK, DQ), bf16),
             pltpu.VMEM((NB, BLK, DQ), bf16),
@@ -468,11 +479,12 @@
             dma((2, NY)),
             dma((NX,)),
             dma((NX,)),
-            dma((NX, 4, 2)),
-            dma((NW,)),
+            dma((NL, 4)),
+            dma((1,)),
             dma((NX, 4)),
-            dma((2, 2)),
             dma((2,)),
+            dma((1,)),
+            dma((NX,)),
             dma((2,)),
             dma((2, NY // 2, NZ)),
             dma((NZ,)),

time: 91 us -> 83.5 us (0.918); the launches traced: 89.3 us -> 83.3 us
  Pallas kernels: 88.7 us -> 82.7 us
    pallas_call x1, Pallas kernels: 86.8 us -> 80.8 us  [shards(): pl.pallas_call(kernel, out_shape=shapes, in_specs=[hbm] * 5, out_specs=(v...]
where the time goes in v3:
time: 83.5 us; the launch traced here: 83.3 us
  Pallas kernels  82.7 us (99%)
    pallas_call x1, Pallas kernels, shards(): pl.pallas_call(kernel, out_shape=shapes, in_specs=[hbm] * 5, out_specs=(v...  80.8 us
    pallas_call x1, Pallas kernels, shards(): pl.pallas_call(deliver, out_shape=shapes, in_specs=[vmem] * 3, out_specs=...  1.86 us

profile of v3, /device:TPU:6, one launch (start us, length us, event | category | flops | bytes accessed | tf_op | source)
XLA Modules:
  0.0 83.3 jit_solution(15319487359396168559)
XLA Ops:
  0.6 80.8 %ffn_backward.1 = (bf16[4,5120]{1,0:T(4,128)(2,1)}, bf16[288,320]{1,0:T(8,128)(2,1)}, bf16[288,320]{1,0:T(8,128)(2,1)}) custom-call(bf16[4,5120]{1,0:T(4,128)(2,1)} %go_ref.1, bf16[4,5120]{1,0:T(4,128)(2,1)} %ti_ref.1, bf16[192,288]{1,0:T(8,128)(2,1)} %pre_ref.1, bf16[288,5120]{1,0:T(8,128)(2,1)} %wo_ref.1, bf16[288,5120]{1,0:T(8,128)(2,1)} %bitcast.2), custom_call_target="tpu_custom_call" | custom-call | flops 2264924160 | bytes 4194304 | tf_op jit(solution)/shard_map/ffn_backward/pallas_call | solution.py:439
  81.5 1.9 %deliver.1 = (bf16[4,5120]{1,0:T(4,128)(2,1)}, bf16[288,320]{1,0:T(8,128)(2,1)}, bf16[288,320]{1,0:T(8,128)(2,1)}) custom-call(bf16[4,5120]{1,0:T(4,128)(2,1)} %get-tuple-element.9.a_ref, bf16[288,320]{1,0:T(8,128)(2,1)} %get-tuple-element.10.b_ref, bf16[288,320]{1,0:T(8,128)(2,1)} %get-tuple-element.11.d_ref), custom_call_target="tpu_custom_call" | custom-call | tf_op jit(solution)/shard_map/deliver/pallas_call | solution.py:500

commit v4 on v3

--- a/solution.py
+++ b/solution.py
@@ -324,21 +324,24 @@
     scale_back = 1.0 / math.sqrt(NL * NX * NC * NB * ROWS)
 
     def weight_parts(a, lhs, right):
-        for h in range(2):
-            some = slice(2 * h * DP, 2 * (h + 1) * DP)
+        for i in range(2):
+            h = 1 - zl // 2 if i == 0 else zl // 2
+            some = pl.ds(pl.multiple_of(2 * DP * h, 128), 2 * DP)
             rows = right[..., some].reshape(NX * QR, 2 * DP)
             part = scale_back * lax.dot_general(
                 lhs, rows, (((0,), (0,)), ((), ())), preferred_element_type=f32
             )
             for k in range(2):
                 put_chunk(a, 2 * h + k, part[:, k * DP : (k + 1) * DP])
+            if a == 1 and i == 0:
+                send(wchunk.at[a, far_near], wpair.at[1], wp_sem.at[1], at(zl_=near))
 
     def put_chunk(a, k, piece):
-        wchunk[a, k] = jnp.concatenate([piece[: HID // 2], piece[HID // 2 :]], axis=1).astype(bf16)
+        whole = jnp.concatenate([piece[: HID // 2], piece[HID // 2 :]], axis=1).astype(bf16)
+        wchunk[a, pl.ds(k, 1)] = whole[None]
 
     def weight_pair(a):
         dev = at(zl_=near)
-        send(wchunk.at[a, far_near], wpair.at[1], wp_sem.at[1], dev)
         send(wchunk.at[a, near], wpair.at[0], wp_sem.at[0], dev)
 
     def weight_far(a):

time: 83.5 us -> 83 us (level)
  no operation moved by 1% of the time
where the time goes in v4:
time: 83 us; the launch traced here: 82.8 us
  Pallas kernels  82.2 us (99%)
    pallas_call x1, Pallas kernels, shards(): pl.pallas_call(kernel, out_shape=shapes, in_specs=[hbm] * 5, out_specs=(v...  80.3 us
    pallas_call x1, Pallas kernels, shards(): pl.pallas_call(deliver, out_shape=shapes, in_specs=[vmem] * 3, out_specs=...  1.86 us

profile of v4, /device:TPU:6, one launch (start us, length us, event | category | flops | bytes accessed | tf_op | source)
XLA Modules:
  0.0 82.8 jit_solution(885990669355624912)
XLA Ops:
  0.6 80.3 %ffn_backward.1 = (bf16[4,5120]{1,0:T(4,128)(2,1)}, bf16[288,320]{1,0:T(8,128)(2,1)}, bf16[288,320]{1,0:T(8,128)(2,1)}) custom-call(bf16[4,5120]{1,0:T(4,128)(2,1)} %go_ref.1, bf16[4,5120]{1,0:T(4,128)(2,1)} %ti_ref.1, bf16[192,288]{1,0:T(8,128)(2,1)} %pre_ref.1, bf16[288,5120]{1,0:T(8,128)(2,1)} %wo_ref.1, bf16[288,5120]{1,0:T(8,128)(2,1)} %bitcast.2), custom_call_target="tpu_custom_call" | custom-call | flops 2264924160 | bytes 4194304 | tf_op jit(solution)/shard_map/ffn_backward/pallas_call | solution.py:442
  81.0 1.9 %deliver.1 = (bf16[4,5120]{1,0:T(4,128)(2,1)}, bf16[288,320]{1,0:T(8,128)(2,1)}, bf16[288,320]{1,0:T(8,128)(2,1)}) custom-call(bf16[4,5120]{1,0:T(4,128)(2,1)} %get-tuple-element.9.a_ref, bf16[288,320]{1,0:T(8,128)(2,1)} %get-tuple-element.10.b_ref, bf16[288,320]{1,0:T(8,128)(2,1)} %get-tuple-element.11.d_ref), custom_call_target="tpu_custom_call" | custom-call | tf_op jit(solution)/shard_map/deliver/pallas_call | solution.py:503
